TPU v7x, 32 devices: a whole 2x2x4 slice. The times are simulated.
32 devices in a mesh: gx: 2 (over core), gy: 4 (over z), gz: 4 (over y, x).
Axes of the slice: x: 2, y: 2, z: 4, core: 2. Of those that a mesh axis runs over, the one named last changes fastest.
Arguments:
- gauge_links: float32 [4, 3, 3, 2, 4, 8, 4, 128], P(None, None, None, None, 'gx', 'gy', 'gz'), may hold values from -1 to 1, as said below
- momenta: float32 [4, 3, 3, 2, 4, 8, 4, 128], P(None, None, None, None, 'gx', 'gy', 'gz'), may hold values from -6 to 6, as said below
Outputs:
- new_links: float32 [4, 3, 3, 2, 4, 8, 4, 128], P(None, None, None, None, 'gx', 'gy', 'gz')
- new_momenta: float32 [4, 3, 3, 2, 4, 8, 4, 128], P(None, None, None, None, 'gx', 'gy', 'gz')
Inputs may be any that keep to these rules, and one draw needn't show every extreme that they name: `gauge_links`: every link is a unitary 3 x 3 matrix of determinant one. `momenta`: every momentum is an anti-Hermitian 3 x 3 matrix of trace zero.
All inputs are finite; a program needn't handle non-finite values.
Results may differ from a plain program's by a relative error of at most 0.0001.
Values sent between devices are 32-bit elements; how exact they have to be, the bound alone decides.
A program may use at most 64 MiB of HBM per device.

v0:
```python
import jax
import jax.numpy as jnp
from jax import lax
from jax.sharding import PartitionSpec as P

BETA = 5.7
STEP = 0.25


def shifted(value, axis, steps):
    count = lax.axis_size(axis)
    pairs = [(source, (source + steps) % count) for source in range(count)]
    return lax.ppermute(value, axis, pairs)


def product(left, right):
    left_real = left[:, :, 0]
    left_imag = left[:, :, 1]
    right_real = right[:, :, 0]
    right_imag = right[:, :, 1]
    real_part = jnp.sum(
        left_real[:, :, None] * right_real[None] - left_imag[:, :, None] * right_imag[None], axis=1
    )
    imag_part = jnp.sum(
        left_real[:, :, None] * right_imag[None] + left_imag[:, :, None] * right_real[None], axis=1
    )
    return jnp.stack([real_part, imag_part], axis=2)


def dagger(matrix):
    return jnp.stack(
        [jnp.swapaxes(matrix[:, :, 0], 0, 1), -jnp.swapaxes(matrix[:, :, 1], 0, 1)], axis=2
    )


def add_identity(matrix):
    identity = jnp.eye(3, dtype=jnp.float32).reshape((3, 3) + (1,) * (matrix.ndim - 3))
    return jnp.stack([matrix[:, :, 0] + identity, matrix[:, :, 1]], axis=2)


def exponent(generator):
    series = add_identity(generator / 4.0)
    series = add_identity(product(generator, series) / 3.0)
    series = add_identity(product(generator, series) / 2.0)
    return add_identity(product(generator, series))


def project(omega):
    real_part = 0.5 * (omega[:, :, 0] - jnp.swapaxes(omega[:, :, 0], 0, 1))
    imag_part = 0.5 * (omega[:, :, 1] + jnp.swapaxes(omega[:, :, 1], 0, 1))
    trace = (omega[0, 0, 1] + omega[1, 1, 1] + omega[2, 2, 1]) / 3.0
    identity = jnp.eye(3, dtype=jnp.float32).reshape((3, 3) + (1,) * trace.ndim)
    imag_part = imag_part - identity * trace
    return jnp.stack([real_part, imag_part], axis=2)


def send_ahead(slab, axis):
    if axis == 0:
        return shifted(slab, "gx", -1)
    if axis == 1:
        return shifted(slab, "gy", -1)
    return shifted(slab, "gz", -1)


def send_back(slab, axis):
    if axis == 0:
        return shifted(slab, "gx", 1)
    if axis == 1:
        return shifted(slab, "gy", 1)
    return shifted(slab, "gz", 1)


def ahead_faces(field):
    faces = {}
    for axis in range(3):
        others = [direction for direction in range(4) if direction != axis]
        slab = jnp.stack(
            [lax.slice_in_dim(field[direction], 0, 1, axis=3 + axis) for direction in others]
        )
        received = send_ahead(slab, axis)
        faces[axis] = {direction: received[number] for number, direction in enumerate(others)}
    return faces


def ahead_link(field, faces, direction, axis):
    if axis == 3:
        return jnp.roll(field[direction], -1, axis=6)
    extent = field[direction].shape[3 + axis]
    inner = lax.slice_in_dim(field[direction], 1, extent, axis=3 + axis)
    return jnp.concatenate([inner, faces[axis][direction]], axis=3 + axis)


def returned_forces(field):
    faces = ahead_faces(field)
    uppers = {}
    lower_sites = {}
    for along in range(4):
        for across in range(4):
            if across == along:
                continue
            step_along = ahead_link(field, faces, across, along)
            step_across = ahead_link(field, faces, along, across)
            uppers[along, across] = product(
                product(step_along, dagger(step_across)), dagger(field[across])
            )
            lower_sites[along, across] = product(
                product(dagger(step_along), dagger(field[along])), field[across]
            )
    lowers = {}
    for across in range(4):
        alongs = [along for along in range(4) if along != across]
        if across == 3:
            for along in alongs:
                lowers[along, across] = jnp.roll(lower_sites[along, across], 1, axis=6)
            continue
        extent = field[0].shape[3 + across]
        slab = jnp.stack(
            [
                lax.slice_in_dim(lower_sites[along, across], extent - 1, extent, axis=3 + across)
                for along in alongs
            ]
        )
        received = send_back(slab, across)
        for number, along in enumerate(alongs):
            inner = lax.slice_in_dim(lower_sites[along, across], 0, extent - 1, axis=3 + across)
            lowers[along, across] = jnp.concatenate([received[number], inner], axis=3 + across)
    result = []
    for along in range(4):
        running = jnp.zeros_like(field[along])
        for across in range(4):
            if across == along:
                continue
            running = running + uppers[along, across] + lowers[along, across]
        omega = product(field[along], running)
        result.append(BETA / 3.0 * project(omega))
    return result


def forces(field):
    return returned_forces(field)


def body(gauge_links, momenta):
    field = [gauge_links[direction] for direction in range(4)]
    moment = [momenta[direction] for direction in range(4)]
    kick = forces(field)
    moment = [moment[direction] - 0.5 * STEP * kick[direction] for direction in range(4)]
    for repeat in range(2):
        field = [
            product(exponent(STEP * moment[direction]), field[direction]) for direction in range(4)
        ]
        kick = forces(field)
        factor = STEP if repeat == 0 else 0.5 * STEP
        moment = [moment[direction] - factor * kick[direction] for direction in range(4)]
    return (jnp.stack(field), jnp.stack(moment))


def solution(mesh):
    placed = (
        P(None, None, None, None, "gx", "gy", "gz", None),
        P(None, None, None, None, "gx", "gy", "gz", None),
    )
    return jax.shard_map(
        body,
        mesh=mesh,
        in_specs=placed,
        out_specs=(
            P(None, None, None, None, "gx", "gy", "gz", None),
            P(None, None, None, None, "gx", "gy", "gz", None),
        ),
        check_vma=False,
    )
```

profile of v0, /device:TPU:0, one launch (start us, length us, event | category | flops | bytes accessed | tf_op | source)
XLA Modules:
  0.0 86.2 jit_solution(12583009588296583655)
XLA Ops:
  0.6 0.8 fusion.286
  1.6 5.1 %collective-permute-start.1 = (f32[3,3,3,2,2,1,1,128]{7,3,2,1,4,6,5,0:T(2,128)S(1)}, f32[3,3,3,2,2,1,1,128]{7,3,2,1,4,6,5,0:T(2,128)S(1)}, u32[]{:S(2)}, u32[]{:S(2)}) collective-permute-start(f32[3,3,3,2,2,1,1,128]{7,3,2,1,4,6,5,0:T(2,128)S(1)} %pad_maximum_fusion.9), channel_id=1, source_target_pairs={{0,12},{4,0},{8,4},{12,8},{1,13},{5,1},{9,5},{13,9},{2,14},{6,2},{... | collective-permute-start | bytes 165896 | tf_op jit(solution)/shard_map/ppermute | solution.py:13
  7.1 2.5 %collective-permute-start.2 = (f32[3,3,3,2,2,2,1,128]{7,6,5,4,3,2,1,0:T(1,128)S(1)}, f32[3,3,3,2,2,2,1,128]{7,6,5,4,3,2,1,0:T(1,128)S(1)}, u32[]{:S(2)}, u32[]{:S(2)}) collective-permute-start(f32[3,3,3,2,2,2,1,128]{7,6,5,4,3,2,1,0:T(1,128)S(1)} %pad_maximum_fusion.2), channel_id=1, source_target_pairs={{0,3},{1,0},{2,1},{3,2},{4,7},{5,4},{6,5},{7,6},{8,11},{9,8},{10,9... | collective-permute-start | bytes 331784 | tf_op jit(solution)/shard_map/ppermute | solution.py:13
  10.0 0.8 copy-done.1
  17.4 2.1 %collective-permute-start.4 = (f32[3,3,3,2,2,2,1,128]{7,5,4,2,1,3,6,0:T(2,128)S(1)}, f32[3,3,3,2,2,2,1,128]{7,5,4,2,1,3,6,0:T(2,128)S(1)}, u32[]{:S(2)}, u32[]{:S(2)}) collective-permute-start(f32[3,3,3,2,2,2,1,128]{7,5,4,2,1,3,6,0:T(2,128)S(1)} %pad_maximum_fusion.3), channel_id=1, source_target_pairs={{0,1},{1,2},{2,3},{3,0},{4,5},{5,6},{6,7},{7,4},{8,9},{9,10},{10,1... | collective-permute-start | bytes 331784 | tf_op jit(solution)/shard_map/ppermute | solution.py:13
  20.2 4.0 %collective-permute-done.4 = f32[3,3,3,2,2,2,1,128]{7,5,4,2,1,3,6,0:T(2,128)S(1)} collective-permute-done((f32[3,3,3,2,2,2,1,128]{7,5,4,2,1,3,6,0:T(2,128)S(1)}, f32[3,3,3,2,2,2,1,128]{7,5,4,2,1,3,6,0:T(2,128)S(1)}, u32[]{:S(2)}, u32[]{:S(2)}) %collective-permute-start.4) | collective-permute-done | bytes 110624 | tf_op jit(solution)/shard_map/ppermute | solution.py:13
  26.6 5.7 %collective-permute-done.3 = f32[3,3,3,2,2,1,1,128]{7,4,2,1,3,6,5,0:T(2,128)S(1)} collective-permute-done((f32[3,3,3,2,2,1,1,128]{7,4,2,1,3,6,5,0:T(2,128)S(1)}, f32[3,3,3,2,2,1,1,128]{7,4,2,1,3,6,5,0:T(2,128)S(1)}, u32[]{:S(2)}, u32[]{:S(2)}) %collective-permute-start.3) | collective-permute-done | bytes 55328 | tf_op jit(solution)/shard_map/ppermute | solution.py:13
  36.7 1.8 %collective-permute-start.8 = (f32[3,3,3,2,2,2,1,128]{7,4,2,1,3,5,6,0:T(2,128)S(1)}, f32[3,3,3,2,2,2,1,128]{7,4,2,1,3,5,6,0:T(2,128)S(1)}, u32[]{:S(2)}, u32[]{:S(2)}) collective-permute-start(f32[3,3,3,2,2,2,1,128]{7,4,2,1,3,5,6,0:T(2,128)S(1)} %pad_maximum_fusion.4), channel_id=1, source_target_pairs={{0,3},{1,0},{2,1},{3,2},{4,7},{5,4},{6,5},{7,6},{8,11},{9,8},{10,9... | collective-permute-start | bytes 331784 | tf_op jit(solution)/shard_map/ppermute | solution.py:13
  38.5 2.2 %collective-permute-done.7 = f32[3,3,3,2,2,1,1,128]{7,4,2,1,3,6,5,0:T(2,128)S(1)} collective-permute-done((f32[3,3,3,2,2,1,1,128]{7,4,2,1,3,6,5,0:T(2,128)S(1)}, f32[3,3,3,2,2,1,1,128]{7,4,2,1,3,6,5,0:T(2,128)S(1)}, u32[]{:S(2)}, u32[]{:S(2)}) %collective-permute-start.7) | collective-permute-done | bytes 55328 | tf_op jit(solution)/shard_map/ppermute | solution.py:13
  43.4 0.7 subtract_reduce_fusion.102
  46.1 2.1 %collective-permute-start.9 = (f32[3,3,3,2,2,1,1,128]{7,4,2,1,3,6,5,0:T(2,128)S(1)}, f32[3,3,3,2,2,1,1,128]{7,4,2,1,3,6,5,0:T(2,128)S(1)}, u32[]{:S(2)}, u32[]{:S(2)}) collective-permute-start(f32[3,3,3,2,2,1,1,128]{7,4,2,1,3,6,5,0:T(2,128)S(1)} %pad_maximum_fusion.14), channel_id=1, source_target_pairs={{0,4},{4,8},{8,12},{12,0},{1,5},{5,9},{9,13},{13,1},{2,6},{6,10},{... | collective-permute-start | bytes 165896 | tf_op jit(solution)/shard_map/ppermute | solution.py:13
  49.6 2.0 %collective-permute-start.10 = (f32[3,3,3,2,2,2,1,128]{7,5,4,2,1,3,6,0:T(2,128)S(1)}, f32[3,3,3,2,2,2,1,128]{7,5,4,2,1,3,6,0:T(2,128)S(1)}, u32[]{:S(2)}, u32[]{:S(2)}) collective-permute-start(f32[3,3,3,2,2,2,1,128]{7,5,4,2,1,3,6,0:T(2,128)S(1)} %pad_maximum_fusion.5), channel_id=1, source_target_pairs={{0,1},{1,2},{2,3},{3,0},{4,5},{5,6},{6,7},{7,4},{8,9},{9,10},{10,1... | collective-permute-start | bytes 331784 | tf_op jit(solution)/shard_map/ppermute | solution.py:13
  52.2 3.4 %collective-permute-done.10 = f32[3,3,3,2,2,2,1,128]{7,5,4,2,1,3,6,0:T(2,128)S(1)} collective-permute-done((f32[3,3,3,2,2,2,1,128]{7,5,4,2,1,3,6,0:T(2,128)S(1)}, f32[3,3,3,2,2,2,1,128]{7,5,4,2,1,3,6,0:T(2,128)S(1)}, u32[]{:S(2)}, u32[]{:S(2)}) %collective-permute-start.10) | collective-permute-done | bytes 110624 | tf_op jit(solution)/shard_map/ppermute | solution.py:13
  57.7 1.0 %collective-permute-done.11 = f32[3,3,3,2,1,2,1,128]{7,5,2,1,3,6,4,0:T(2,128)S(1)} collective-permute-done((f32[3,3,3,2,1,2,1,128]{7,5,2,1,3,6,4,0:T(2,128)S(1)}, f32[3,3,3,2,1,2,1,128]{7,5,2,1,3,6,4,0:T(2,128)S(1)}, u32[]{:S(2)}, u32[]{:S(2)}) %collective-permute-start.11) | collective-permute-done | bytes 55328 | tf_op jit(solution)/shard_map/ppermute | solution.py:13
  63.0 1.9 %collective-permute-start.13 = (f32[3,3,3,2,2,1,1,128]{7,4,2,1,3,6,5,0:T(2,128)S(1)}, f32[3,3,3,2,2,1,1,128]{7,4,2,1,3,6,5,0:T(2,128)S(1)}, u32[]{:S(2)}, u32[]{:S(2)}) collective-permute-start(f32[3,3,3,2,2,1,1,128]{7,4,2,1,3,6,5,0:T(2,128)S(1)} %pad_maximum_fusion.17), channel_id=1, source_target_pairs={{0,12},{4,0},{8,4},{12,8},{1,13},{5,1},{9,5},{13,9},{2,14},{6,2},{... | collective-permute-start | bytes 165896 | tf_op jit(solution)/shard_map/ppermute | solution.py:13
  65.2 0.8 copy.5647
  66.0 1.7 %collective-permute-start.14 = (f32[3,3,3,2,2,2,1,128]{7,5,4,2,1,3,6,0:T(2,128)S(1)}, f32[3,3,3,2,2,2,1,128]{7,5,4,2,1,3,6,0:T(2,128)S(1)}, u32[]{:S(2)}, u32[]{:S(2)}) collective-permute-start(f32[3,3,3,2,2,2,1,128]{7,5,4,2,1,3,6,0:T(2,128)S(1)} %pad_maximum_fusion.6), channel_id=1, source_target_pairs={{0,3},{1,0},{2,1},{3,2},{4,7},{5,4},{6,5},{7,6},{8,11},{9,8},{10,9... | collective-permute-start | bytes 331784 | tf_op jit(solution)/shard_map/ppermute | solution.py:13
  68.7 2.3 %collective-permute-done.14 = f32[3,3,3,2,2,2,1,128]{7,5,4,2,1,3,6,0:T(2,128)S(1)} collective-permute-done((f32[3,3,3,2,2,2,1,128]{7,5,4,2,1,3,6,0:T(2,128)S(1)}, f32[3,3,3,2,2,2,1,128]{7,5,4,2,1,3,6,0:T(2,128)S(1)}, u32[]{:S(2)}, u32[]{:S(2)}) %collective-permute-start.14) | collective-permute-done | bytes 110624 | tf_op jit(solution)/shard_map/ppermute | solution.py:13
  72.6 0.7 subtract_reduce_fusion.42
  76.3 1.7 %collective-permute-start.16 = (f32[3,3,3,2,2,2,1,128]{7,5,4,2,1,3,6,0:T(2,128)S(1)}, f32[3,3,3,2,2,2,1,128]{7,5,4,2,1,3,6,0:T(2,128)S(1)}, u32[]{:S(2)}, u32[]{:S(2)}) collective-permute-start(f32[3,3,3,2,2,2,1,128]{7,5,4,2,1,3,6,0:T(2,128)S(1)} %pad_maximum_fusion.7), channel_id=1, source_target_pairs={{0,1},{1,2},{2,3},{3,0},{4,5},{5,6},{6,7},{7,4},{8,9},{9,10},{10,1... | collective-permute-start | bytes 331784 | tf_op jit(solution)/shard_map/ppermute | solution.py:13
  78.1 2.6 %collective-permute-done.15 = f32[3,3,3,2,2,1,1,128]{7,4,2,1,3,6,5,0:T(2,128)S(1)} collective-permute-done((f32[3,3,3,2,2,1,1,128]{7,4,2,1,3,6,5,0:T(2,128)S(1)}, f32[3,3,3,2,2,1,1,128]{7,4,2,1,3,6,5,0:T(2,128)S(1)}, u32[]{:S(2)}, u32[]{:S(2)}) %collective-permute-start.15) | collective-permute-done | bytes 55328 | tf_op jit(solution)/shard_map/ppermute | solution.py:13
  80.7 1.4 %collective-permute-done.16 = f32[3,3,3,2,2,2,1,128]{7,5,4,2,1,3,6,0:T(2,128)S(1)} collective-permute-done((f32[3,3,3,2,2,2,1,128]{7,5,4,2,1,3,6,0:T(2,128)S(1)}, f32[3,3,3,2,2,2,1,128]{7,5,4,2,1,3,6,0:T(2,128)S(1)}, u32[]{:S(2)}, u32[]{:S(2)}) %collective-permute-start.16) | collective-permute-done | bytes 110624 | tf_op jit(solution)/shard_map/ppermute | solution.py:13
  82.8 1.2 %collective-permute-done.17 = f32[3,3,3,2,1,2,1,128]{7,5,2,1,3,6,4,0:T(2,128)S(1)} collective-permute-done((f32[3,3,3,2,1,2,1,128]{7,5,2,1,3,6,4,0:T(2,128)S(1)}, f32[3,3,3,2,1,2,1,128]{7,5,2,1,3,6,4,0:T(2,128)S(1)}, u32[]{:S(2)}, u32[]{:S(2)}) %collective-permute-start.17) | collective-permute-done | bytes 55328 | tf_op jit(solution)/shard_map/ppermute | solution.py:13
  85.4 0.8 copy.5648
  (607 shorter events, 32.5 us)
Async XLA Ops:
  1.6 5.2 %copy-start = (f32[4,3,3,2,2,2,1,128]{7,6,5,4,3,2,1,0:T(1,128)S(1)}, f32[4,3,3,2,2,2,1,128]{7,6,5,4,3,2,1,0:T(1,128)}, u32[]{:S(2)}) copy-start(f32[4,3,3,2,2,2,1,128]{7,6,5,4,3,2,1,0:T(1,128)} %param.2) | copy-start | bytes 442372
  1.6 10.0 %collective-permute-start.1 = (f32[3,3,3,2,2,1,1,128]{7,3,2,1,4,6,5,0:T(2,128)S(1)}, f32[3,3,3,2,2,1,1,128]{7,3,2,1,4,6,5,0:T(2,128)S(1)}, u32[]{:S(2)}, u32[]{:S(2)}) collective-permute-start(f32[3,3,3,2,2,1,1,128]{7,3,2,1,4,6,5,0:T(2,128)S(1)} %pad_maximum_fusion.9), channel_id=1, source_target_pairs={{0,12},{4,0},{8,4},{12,8},{1,13},{5,1},{9,5},{13,9},{2,14},{6,2},{... | collective-permute-start | bytes 165896 | tf_op jit(solution)/shard_map/ppermute | solution.py:13
  6.9 5.0 %collective-permute-start = (f32[3,3,3,2,1,2,1,128]{7,5,3,2,1,6,4,0:T(2,128)S(1)}, f32[3,3,3,2,1,2,1,128]{7,5,3,2,1,6,4,0:T(2,128)S(1)}, u32[]{:S(2)}, u32[]{:S(2)}) collective-permute-start(f32[3,3,3,2,1,2,1,128]{7,5,3,2,1,6,4,0:T(2,128)S(1)} %pad_maximum_fusion.8), channel_id=1, source_target_pairs={{0,16},{16,0},{1,17},{17,1},{2,18},{18,2},{3,19},{19,3},{4,20},{20... | collective-permute-start | bytes 165896 | tf_op jit(solution)/shard_map/ppermute | solution.py:13
  7.1 5.6 %collective-permute-start.2 = (f32[3,3,3,2,2,2,1,128]{7,6,5,4,3,2,1,0:T(1,128)S(1)}, f32[3,3,3,2,2,2,1,128]{7,6,5,4,3,2,1,0:T(1,128)S(1)}, u32[]{:S(2)}, u32[]{:S(2)}) collective-permute-start(f32[3,3,3,2,2,2,1,128]{7,6,5,4,3,2,1,0:T(1,128)S(1)} %pad_maximum_fusion.2), channel_id=1, source_target_pairs={{0,3},{1,0},{2,1},{3,2},{4,7},{5,4},{6,5},{7,6},{8,11},{9,8},{10,9... | collective-permute-start | bytes 331784 | tf_op jit(solution)/shard_map/ppermute | solution.py:13
  9.9 0.9 %copy-start.1 = (f32[4,3,3,2,2,2,1,128]{7,6,5,4,3,2,1,0:T(1,128)S(1)}, f32[4,3,3,2,2,2,1,128]{7,6,5,4,3,2,1,0:T(1,128)}, u32[]{:S(2)}) copy-start(f32[4,3,3,2,2,2,1,128]{7,6,5,4,3,2,1,0:T(1,128)} %param.3) | copy-start | bytes 442372
  16.7 3.4 %collective-permute-start.5 = (f32[3,3,3,2,1,2,1,128]{7,5,2,1,3,6,4,0:T(2,128)S(1)}, f32[3,3,3,2,1,2,1,128]{7,5,2,1,3,6,4,0:T(2,128)S(1)}, u32[]{:S(2)}, u32[]{:S(2)}) collective-permute-start(f32[3,3,3,2,1,2,1,128]{7,5,2,1,3,6,4,0:T(2,128)S(1)} %pad_maximum_fusion.11), channel_id=1, source_target_pairs={{0,16},{16,0},{1,17},{17,1},{2,18},{18,2},{3,19},{19,3},{4,20},{20... | collective-permute-start | bytes 165896 | tf_op jit(solution)/shard_map/ppermute | solution.py:13
  17.4 6.8 %collective-permute-start.4 = (f32[3,3,3,2,2,2,1,128]{7,5,4,2,1,3,6,0:T(2,128)S(1)}, f32[3,3,3,2,2,2,1,128]{7,5,4,2,1,3,6,0:T(2,128)S(1)}, u32[]{:S(2)}, u32[]{:S(2)}) collective-permute-start(f32[3,3,3,2,2,2,1,128]{7,5,4,2,1,3,6,0:T(2,128)S(1)} %pad_maximum_fusion.3), channel_id=1, source_target_pairs={{0,1},{1,2},{2,3},{3,0},{4,5},{5,6},{6,7},{7,4},{8,9},{9,10},{10,1... | collective-permute-start | bytes 331784 | tf_op jit(solution)/shard_map/ppermute | solution.py:13
  26.1 6.2 %collective-permute-start.3 = (f32[3,3,3,2,2,1,1,128]{7,4,2,1,3,6,5,0:T(2,128)S(1)}, f32[3,3,3,2,2,1,1,128]{7,4,2,1,3,6,5,0:T(2,128)S(1)}, u32[]{:S(2)}, u32[]{:S(2)}) collective-permute-start(f32[3,3,3,2,2,1,1,128]{7,4,2,1,3,6,5,0:T(2,128)S(1)} %pad_maximum_fusion.10), channel_id=1, source_target_pairs={{0,4},{4,8},{8,12},{12,0},{1,5},{5,9},{9,13},{13,1},{2,6},{6,10},{... | collective-permute-start | bytes 165896 | tf_op jit(solution)/shard_map/ppermute | solution.py:13
  36.5 4.2 %collective-permute-start.7 = (f32[3,3,3,2,2,1,1,128]{7,4,2,1,3,6,5,0:T(2,128)S(1)}, f32[3,3,3,2,2,1,1,128]{7,4,2,1,3,6,5,0:T(2,128)S(1)}, u32[]{:S(2)}, u32[]{:S(2)}) collective-permute-start(f32[3,3,3,2,2,1,1,128]{7,4,2,1,3,6,5,0:T(2,128)S(1)} %pad_maximum_fusion.13), channel_id=1, source_target_pairs={{0,12},{4,0},{8,4},{12,8},{1,13},{5,1},{9,5},{13,9},{2,14},{6,2},{... | collective-permute-start | bytes 165896 | tf_op jit(solution)/shard_map/ppermute | solution.py:13
  36.6 4.3 %collective-permute-start.6 = (f32[3,3,3,2,1,2,1,128]{7,5,3,2,1,6,4,0:T(2,128)S(1)}, f32[3,3,3,2,1,2,1,128]{7,5,3,2,1,6,4,0:T(2,128)S(1)}, u32[]{:S(2)}, u32[]{:S(2)}) collective-permute-start(f32[3,3,3,2,1,2,1,128]{7,5,3,2,1,6,4,0:T(2,128)S(1)} %pad_maximum_fusion.12), channel_id=1, source_target_pairs={{0,16},{16,0},{1,17},{17,1},{2,18},{18,2},{3,19},{19,3},{4,20},{20... | collective-permute-start | bytes 165896 | tf_op jit(solution)/shard_map/ppermute | solution.py:13
  36.7 5.5 %collective-permute-start.8 = (f32[3,3,3,2,2,2,1,128]{7,4,2,1,3,5,6,0:T(2,128)S(1)}, f32[3,3,3,2,2,2,1,128]{7,4,2,1,3,5,6,0:T(2,128)S(1)}, u32[]{:S(2)}, u32[]{:S(2)}) collective-permute-start(f32[3,3,3,2,2,2,1,128]{7,4,2,1,3,5,6,0:T(2,128)S(1)} %pad_maximum_fusion.4), channel_id=1, source_target_pairs={{0,3},{1,0},{2,1},{3,2},{4,7},{5,4},{6,5},{7,6},{8,11},{9,8},{10,9... | collective-permute-start | bytes 331784 | tf_op jit(solution)/shard_map/ppermute | solution.py:13
  46.1 6.0 %collective-permute-start.9 = (f32[3,3,3,2,2,1,1,128]{7,4,2,1,3,6,5,0:T(2,128)S(1)}, f32[3,3,3,2,2,1,1,128]{7,4,2,1,3,6,5,0:T(2,128)S(1)}, u32[]{:S(2)}, u32[]{:S(2)}) collective-permute-start(f32[3,3,3,2,2,1,1,128]{7,4,2,1,3,6,5,0:T(2,128)S(1)} %pad_maximum_fusion.14), channel_id=1, source_target_pairs={{0,4},{4,8},{8,12},{12,0},{1,5},{5,9},{9,13},{13,1},{2,6},{6,10},{... | collective-permute-start | bytes 165896 | tf_op jit(solution)/shard_map/ppermute | solution.py:13
  49.6 5.9 %collective-permute-start.10 = (f32[3,3,3,2,2,2,1,128]{7,5,4,2,1,3,6,0:T(2,128)S(1)}, f32[3,3,3,2,2,2,1,128]{7,5,4,2,1,3,6,0:T(2,128)S(1)}, u32[]{:S(2)}, u32[]{:S(2)}) collective-permute-start(f32[3,3,3,2,2,2,1,128]{7,5,4,2,1,3,6,0:T(2,128)S(1)} %pad_maximum_fusion.5), channel_id=1, source_target_pairs={{0,1},{1,2},{2,3},{3,0},{4,5},{5,6},{6,7},{7,4},{8,9},{9,10},{10,1... | collective-permute-start | bytes 331784 | tf_op jit(solution)/shard_map/ppermute | solution.py:13
  57.4 1.3 %collective-permute-start.11 = (f32[3,3,3,2,1,2,1,128]{7,5,2,1,3,6,4,0:T(2,128)S(1)}, f32[3,3,3,2,1,2,1,128]{7,5,2,1,3,6,4,0:T(2,128)S(1)}, u32[]{:S(2)}, u32[]{:S(2)}) collective-permute-start(f32[3,3,3,2,1,2,1,128]{7,5,2,1,3,6,4,0:T(2,128)S(1)} %pad_maximum_fusion.15), channel_id=1, source_target_pairs={{0,16},{16,0},{1,17},{17,1},{2,18},{18,2},{3,19},{19,3},{4,20},{20... | collective-permute-start | bytes 165896 | tf_op jit(solution)/shard_map/ppermute | solution.py:13
  62.8 4.9 %collective-permute-start.12 = (f32[3,3,3,2,1,2,1,128]{7,5,2,1,3,6,4,0:T(2,128)S(1)}, f32[3,3,3,2,1,2,1,128]{7,5,2,1,3,6,4,0:T(2,128)S(1)}, u32[]{:S(2)}, u32[]{:S(2)}) collective-permute-start(f32[3,3,3,2,1,2,1,128]{7,5,2,1,3,6,4,0:T(2,128)S(1)} %pad_maximum_fusion.16), channel_id=1, source_target_pairs={{0,16},{16,0},{1,17},{17,1},{2,18},{18,2},{3,19},{19,3},{4,20},{20... | collective-permute-start | bytes 165896 | tf_op jit(solution)/shard_map/ppermute | solution.py:13
  63.0 4.9 %collective-permute-start.13 = (f32[3,3,3,2,2,1,1,128]{7,4,2,1,3,6,5,0:T(2,128)S(1)}, f32[3,3,3,2,2,1,1,128]{7,4,2,1,3,6,5,0:T(2,128)S(1)}, u32[]{:S(2)}, u32[]{:S(2)}) collective-permute-start(f32[3,3,3,2,2,1,1,128]{7,4,2,1,3,6,5,0:T(2,128)S(1)} %pad_maximum_fusion.17), channel_id=1, source_target_pairs={{0,12},{4,0},{8,4},{12,8},{1,13},{5,1},{9,5},{13,9},{2,14},{6,2},{... | collective-permute-start | bytes 165896 | tf_op jit(solution)/shard_map/ppermute | solution.py:13
  66.0 5.0 %collective-permute-start.14 = (f32[3,3,3,2,2,2,1,128]{7,5,4,2,1,3,6,0:T(2,128)S(1)}, f32[3,3,3,2,2,2,1,128]{7,5,4,2,1,3,6,0:T(2,128)S(1)}, u32[]{:S(2)}, u32[]{:S(2)}) collective-permute-start(f32[3,3,3,2,2,2,1,128]{7,5,4,2,1,3,6,0:T(2,128)S(1)} %pad_maximum_fusion.6), channel_id=1, source_target_pairs={{0,3},{1,0},{2,1},{3,2},{4,7},{5,4},{6,5},{7,6},{8,11},{9,8},{10,9... | collective-permute-start | bytes 331784 | tf_op jit(solution)/shard_map/ppermute | solution.py:13
  74.6 6.0 %collective-permute-start.15 = (f32[3,3,3,2,2,1,1,128]{7,4,2,1,3,6,5,0:T(2,128)S(1)}, f32[3,3,3,2,2,1,1,128]{7,4,2,1,3,6,5,0:T(2,128)S(1)}, u32[]{:S(2)}, u32[]{:S(2)}) collective-permute-start(f32[3,3,3,2,2,1,1,128]{7,4,2,1,3,6,5,0:T(2,128)S(1)} %pad_maximum_fusion.18), channel_id=1, source_target_pairs={{0,4},{4,8},{8,12},{12,0},{1,5},{5,9},{9,13},{13,1},{2,6},{6,10},{... | collective-permute-start | bytes 165896 | tf_op jit(solution)/shard_map/ppermute | solution.py:13
  76.3 5.7 %collective-permute-start.16 = (f32[3,3,3,2,2,2,1,128]{7,5,4,2,1,3,6,0:T(2,128)S(1)}, f32[3,3,3,2,2,2,1,128]{7,5,4,2,1,3,6,0:T(2,128)S(1)}, u32[]{:S(2)}, u32[]{:S(2)}) collective-permute-start(f32[3,3,3,2,2,2,1,128]{7,5,4,2,1,3,6,0:T(2,128)S(1)} %pad_maximum_fusion.7), channel_id=1, source_target_pairs={{0,1},{1,2},{2,3},{3,0},{4,5},{5,6},{6,7},{7,4},{8,9},{9,10},{10,1... | collective-permute-start | bytes 331784 | tf_op jit(solution)/shard_map/ppermute | solution.py:13
  82.7 1.3 %collective-permute-start.17 = (f32[3,3,3,2,1,2,1,128]{7,5,2,1,3,6,4,0:T(2,128)S(1)}, f32[3,3,3,2,1,2,1,128]{7,5,2,1,3,6,4,0:T(2,128)S(1)}, u32[]{:S(2)}, u32[]{:S(2)}) collective-permute-start(f32[3,3,3,2,1,2,1,128]{7,5,2,1,3,6,4,0:T(2,128)S(1)} %pad_maximum_fusion.19), channel_id=1, source_target_pairs={{0,16},{16,0},{1,17},{17,1},{2,18},{18,2},{3,19},{19,3},{4,20},{20... | collective-permute-start | bytes 165896 | tf_op jit(solution)/shard_map/ppermute | solution.py:13
where the time goes:
time: 86.4 us; the launch traced here: 86.2 us
  other arithmetic  27.5 us (32%)
  waiting for transfers between devices  24.7 us (29%)
  starting transfers between devices  22.2 us (26%)
  local copies, waits for them, and re-layouts  7.24 us (8%)
  between operations  4.55 us (5%)
    ppermute x18, waiting for transfers between devices, shifted(): return lax.ppermute(value, axis, pairs)  24.7 us
    ppermute x18, starting transfers between devices, shifted(): return lax.ppermute(value, axis, pairs)  22.2 us
    reduce_sum x91, other arithmetic, product(): jnp.sum(left_real[:, :, None] * right_real[None] - left_imag[:, :, None]...  16.6 us
    unnamed x23, local copies, waits for them, and re-layouts  2.61 us
    add x26, other arithmetic, add_identity(): return jnp.stack([matrix[:, :, 0] + identity, matrix[:, :, 1]], axis=2)  2.01 us
  transfers between devices with their start and end apart: 18, of which 11 were waited for; matrix products, arithmetic and copies ran while one was open for 10% of the time, Pallas kernels for 0%

commit v1 on v0

v1 whole, which is shorter than its diff:
```python
import jax
import jax.numpy as jnp
from jax import lax
from jax.experimental import pallas as pl
from jax.experimental.pallas import tpu as pltpu
from jax.sharding import PartitionSpec as P

BETA = 5.7
STEP = 0.25
AXES = ("gx", "gy", "gz")
MESH = pl.DeviceIdType.MESH

MOMENT_PLANES = (2, 4, 10, 3, 5, 11, 1, 9)


def matrix(planes):
    return [
        [(planes[(row * 3 + column) * 2], planes[(row * 3 + column) * 2 + 1]) for column in range(3)]
        for row in range(3)
    ]


def dagger(value):
    return ("dagger", value)


def entry(value, row, column):
    if isinstance(value, tuple):
        real, imag = value[1][column][row]
        return real, imag, True
    real, imag = value[row][column]
    return real, imag, False


def product(left, right):
    result = []
    for row in range(3):
        line = []
        for column in range(3):
            real = imag = None
            for inner in range(3):
                lr, li, lc = entry(left, row, inner)
                rr, ri, rc = entry(right, inner, column)
                rr_part = lr * rr
                ii_part = li * ri
                ri_part = lr * ri
                ir_part = li * rr
                first = rr_part - ii_part if lc == rc else rr_part + ii_part
                if real is None:
                    real = first
                    if rc and lc:
                        imag = -(ri_part + ir_part)
                    elif rc:
                        imag = ir_part - ri_part
                    elif lc:
                        imag = ri_part - ir_part
                    else:
                        imag = ri_part + ir_part
                else:
                    real = real + first
                    imag = imag - ri_part if rc else imag + ri_part
                    imag = imag - ir_part if lc else imag + ir_part
            line.append((real, imag))
        result.append(line)
    return result


def project(omega):
    third = (omega[0][0][1] + omega[1][1][1] + omega[2][2][1]) * (1.0 / 3.0)
    return [
        0.5 * (omega[0][1][0] - omega[1][0][0]),
        0.5 * (omega[0][2][0] - omega[2][0][0]),
        0.5 * (omega[1][2][0] - omega[2][1][0]),
        0.5 * (omega[0][1][1] + omega[1][0][1]),
        0.5 * (omega[0][2][1] + omega[2][0][1]),
        0.5 * (omega[1][2][1] + omega[2][1][1]),
        omega[0][0][1] - third,
        omega[1][1][1] - third,
    ]


def exponent(planes):
    r01, r02, r12, s01, s02, s12, s00, s11 = [STEP * plane for plane in planes]
    s22 = -(s00 + s11)
    n01 = s01 * s01 + r01 * r01
    n02 = s02 * s02 + r02 * r02
    n12 = s12 * s12 + r12 * r12
    q00 = s00 * s00 + n01 + n02
    q11 = s11 * s11 + n01 + n12
    q22 = s22 * s22 + n02 + n12
    a_re = s01 * s12 - r01 * r12
    a_im = -(s01 * r12 + r01 * s12)
    q01_re = s02 * s12 + r02 * r12 - s01 * s22
    q01_im = s02 * r12 - r02 * s12 + r01 * s22
    q02_re = a_re - s02 * s11
    q02_im = a_im + r02 * s11
    q12_re = s01 * s02 + r01 * r02 - s12 * s00
    q12_im = r01 * s02 - s01 * r02 + r12 * s00
    half_trace = 0.5 * (q00 + q11 + q22)
    determinant = (
        s00 * (s11 * s22 - n12) - s11 * n02 - s22 * n01 + 2.0 * (a_re * s02 - a_im * r02)
    )
    alpha_im = determinant * (-1.0 / 6.0)
    beta_re = determinant * (1.0 / 24.0)
    beta_im = 1.0 - half_trace * (1.0 / 6.0)
    gamma = half_trace * (1.0 / 24.0) - 0.5

    def diagonal(s, q):
        return 1.0 + beta_re * s + gamma * q, alpha_im + beta_im * s

    def pair(s, r, q_re, q_im):
        even_re = beta_re * s + gamma * q_re
        even_im = gamma * q_im - beta_re * r
        odd_re = beta_im * r
        odd_im = beta_im * s
        upper = (even_re + odd_re, even_im + odd_im)
        lower = (even_re - odd_re, odd_im - even_im)
        return upper, lower

    e01, e10 = pair(s01, r01, q01_re, q01_im)
    e02, e20 = pair(s02, r02, q02_re, q02_im)
    e12, e21 = pair(s12, r12, q12_re, q12_im)
    return [
        [diagonal(s00, q00), e01, e02],
        [e10, diagonal(s11, q11), e12],
        [e20, e21, diagonal(s22, q22)],
    ]


def advance(moment_ref, field_ref):
    step = exponent([moment_ref[plane] for plane in range(8)])
    moved = product(step, matrix([field_ref[plane] for plane in range(18)]))
    for row in range(3):
        for column in range(3):
            for part in range(2):
                field_ref[(row * 3 + column) * 2 + part] = moved[row][column][part]


def kernel(
    links_in, moment_in, links_out, moment_out,
    field, halo, moment, moment_halo, kicks, kicks_in, local, operands, results,
    field_send, field_recv, moment_send, moment_recv, kick_send, kick_recv,
):
    coords = [lax.axis_index(axis) for axis in AXES]
    counts = [lax.axis_size(axis) for axis in AXES]

    def neighbour(axis, steps):
        place = list(coords)
        place[axis] = lax.rem(coords[axis] + (steps + counts[axis]), counts[axis])
        return tuple(place)

    barrier = pltpu.get_barrier_semaphore()
    for axis in range(3):
        for steps in (-1, 1):
            pl.semaphore_signal(barrier, inc=1, device_id=neighbour(axis, steps), device_id_type=MESH)

    for half in range(2):
        field[half] = jnp.concatenate([links_in[2 * half], links_in[2 * half + 1]], axis=1)
        for plane, source in enumerate(MOMENT_PLANES):
            moment[half, plane] = jnp.concatenate(
                [moment_in[2 * half, source], moment_in[2 * half + 1, source]], axis=0
            )
    pl.semaphore_wait(barrier, 6)

    def field_copy(axis):
        return pltpu.make_async_remote_copy(
            src_ref=field, dst_ref=halo.at[axis],
            send_sem=field_send.at[axis], recv_sem=field_recv.at[axis],
            device_id=neighbour(axis, -1), device_id_type=MESH,
        )

    def moment_copy(repeat, axis):
        return pltpu.make_async_remote_copy(
            src_ref=moment, dst_ref=moment_halo.at[repeat, axis],
            send_sem=moment_send.at[repeat, axis], recv_sem=moment_recv.at[repeat, axis],
            device_id=neighbour(axis, -1), device_id_type=MESH,
        )

    def kick_copy(repeat, axis):
        return pltpu.make_async_remote_copy(
            src_ref=kicks.at[axis], dst_ref=kicks_in.at[repeat, axis],
            send_sem=kick_send.at[repeat, axis], recv_sem=kick_recv.at[repeat, axis],
            device_id=neighbour(axis, 1), device_id_type=MESH,
        )

    for axis in (2, 1, 0):
        field_copy(axis).start()

    row = lax.broadcasted_iota(jnp.int32, (1, 8, 128), 1)
    top = row < 4
    near_x = lax.rem(row, 4) < 2
    near_y = lax.rem(row, 2) < 1

    def select(mask, first, second):
        return jnp.where(jnp.broadcast_to(mask, first.shape), first, second)

    def flip(value):
        return pltpu.roll(value, 4, 1)

    def swap_x(value):
        return select(near_x, pltpu.roll(value, 6, 1), pltpu.roll(value, 2, 1))

    def swap_y(value):
        return select(near_y, pltpu.roll(value, 7, 1), pltpu.roll(value, 1, 1))

    def ahead_x(half):
        return swap_x(select(near_x, halo[0, half], field[half]))

    def ahead_y(half):
        return swap_y(select(near_y, halo[1, half], field[half]))

    def ahead_t(half):
        return pltpu.roll(field[half], 127, 2)

    def gather_operands():
        operands[0, 0] = field[0]
        operands[1, 0] = field[0]
        operands[0, 3] = field[1]
        operands[1, 3] = flip(field[1])
        operands[2, 0] = select(top, field[0], flip(field[1]))
        operands[2, 3] = select(top, flip(field[0]), field[1])
        x_one = ahead_x(1)
        y_one = ahead_y(1)
        operands[0, 1] = select(top, x_one, y_one)
        operands[1, 1] = flip(select(top, y_one, x_one))
        operands[2, 1] = select(top, flip(ahead_x(0)), halo[2, 1])
        t_zero = ahead_t(0)
        operands[0, 2] = select(top, halo[2, 0], t_zero)
        operands[1, 2] = select(top, t_zero, halo[2, 0])
        operands[2, 2] = select(top, ahead_y(0), flip(ahead_t(1)))

    def group(number, carry):
        def load(which):
            return matrix([operands[number, which, plane] for plane in range(18)])

        def store(which, value):
            for plane, part in enumerate(project(value)):
                results[number, which, plane] = part

        here, along, across, side = load(0), load(1), load(2), load(3)
        one = product(here, along)
        two = product(side, across)
        store(0, product(one, dagger(two)))
        store(1, product(across, product(dagger(one), side)))
        store(2, product(along, product(dagger(two), here)))
        return carry

    def round_of(repeat, carry):
        gather_operands()
        lax.fori_loop(0, 3, group, 0)

        zero = jnp.zeros((8, 8, 128), jnp.float32)
        nu_a, nu_b, nu_c = results[0, 2], results[1, 2], results[2, 2]
        mu_a, mu_b, mu_c = results[0, 1], results[1, 1], results[2, 1]
        kicks[2, 0] = select(top, mu_a, mu_b)
        kicks[2, 1] = select(top, zero, nu_c)
        kick_copy(repeat, 2).start()
        nu_b = flip(nu_b)
        kicks[1, 0] = select(top, mu_c, zero)
        kicks[1, 1] = select(top, nu_b, nu_a)
        kick_copy(repeat, 1).start()
        kicks[0, 0] = select(top, zero, flip(nu_c))
        kicks[0, 1] = select(top, nu_a, nu_b)
        kick_copy(repeat, 0).start()
        p_a, p_b, p_c = results[0, 0], results[1, 0], results[2, 0]
        q_c = flip(p_c)
        local[0] = (
            p_a + p_b + select(top, p_c, -q_c) + pltpu.roll(select(top, mu_b, mu_a), 1, 2)
        )
        local[1] = (
            select(top, q_c, -p_c) - p_a - flip(p_b)
            + pltpu.roll(select(top, flip(mu_c), zero), 1, 2)
        )
        kick_copy(repeat, 0).wait()
        for half in range(2):
            local[half] += swap_x(select(near_x, kicks[0, half], kicks_in[repeat, 0, half]))
        kick_copy(repeat, 1).wait()
        for half in range(2):
            local[half] += swap_y(select(near_y, kicks[1, half], kicks_in[repeat, 1, half]))
        kick_copy(repeat, 2).wait()
        factor = jnp.where(repeat == 1, STEP * BETA / 3.0, 0.5 * STEP * BETA / 3.0)
        for half in range(2):
            moment[half] = moment[half] - factor * (local[half] + kicks_in[repeat, 2, half])

        @pl.when(repeat < 2)
        def _():
            for axis in (2, 1, 0):
                moment_copy(repeat, axis).start()

            def own(half, carry):
                advance(moment.at[half], field.at[half])
                return carry

            lax.fori_loop(0, 2, own, 0)

            def arrived(axis, carry):
                moment_copy(repeat, axis).wait()

                def ahead(half, carry):
                    advance(moment_halo.at[repeat, axis, half], halo.at[axis, half])
                    return carry

                return lax.fori_loop(0, 2, ahead, carry)

            for axis in range(3):
                arrived(axis, 0)

        return carry

    for axis in range(3):
        field_copy(axis).wait()
    lax.fori_loop(0, 3, round_of, 0)

    for half in range(2):
        for place in range(2):
            rows = slice(4 * place, 4 * place + 4)
            links_out[2 * half + place] = field[half, :, rows, :]
        r01, r02, r12, s01, s02, s12, s00, s11 = [moment[half, plane] for plane in range(8)]
        zero = jnp.zeros_like(r01)
        planes = [
            zero, s00, r01, s01, r02, s02,
            -r01, s01, zero, s11, r12, s12,
            -r02, s02, -r12, s12, zero, -(s00 + s11),
        ]
        for plane, value in enumerate(planes):
            moment_out[2 * half, plane] = value[0:4]
            moment_out[2 * half + 1, plane] = value[4:8]


def body(gauge_links, momenta):
    shape = gauge_links.shape
    assert shape == (4, 3, 3, 2, 2, 2, 1, 128)
    whole = jax.ShapeDtypeStruct((4, 18, 4, 128), jnp.float32)
    vmem = pl.BlockSpec(memory_space=pltpu.VMEM)
    links, moment = pl.pallas_call(
        kernel,
        out_shape=(whole, whole),
        in_specs=[vmem, vmem],
        out_specs=(vmem, vmem),
        scratch_shapes=[
            pltpu.VMEM((2, 18, 8, 128), jnp.float32),
            pltpu.VMEM((3, 2, 18, 8, 128), jnp.float32),
            pltpu.VMEM((2, 8, 8, 128), jnp.float32),
            pltpu.VMEM((2, 3, 2, 8, 8, 128), jnp.float32),
            pltpu.VMEM((3, 2, 8, 8, 128), jnp.float32),
            pltpu.VMEM((3, 3, 2, 8, 8, 128), jnp.float32),
            pltpu.VMEM((2, 8, 8, 128), jnp.float32),
            pltpu.VMEM((3, 4, 18, 8, 128), jnp.float32),
            pltpu.VMEM((3, 3, 8, 8, 128), jnp.float32),
            pltpu.SemaphoreType.DMA((3,)),
            pltpu.SemaphoreType.DMA((3,)),
            pltpu.SemaphoreType.DMA((2, 3)),
            pltpu.SemaphoreType.DMA((2, 3)),
            pltpu.SemaphoreType.DMA((3, 3)),
            pltpu.SemaphoreType.DMA((3, 3)),
        ],
        compiler_params=pltpu.CompilerParams(
            collective_id=0, has_side_effects=True, vmem_limit_bytes=16 * 1024 * 1024
        ),
    )(gauge_links.reshape(4, 18, 4, 128), momenta.reshape(4, 18, 4, 128))
    return links.reshape(shape), moment.reshape(shape)


def solution(mesh):
    spec = P(None, None, None, None, "gx", "gy", "gz", None)
    return jax.shard_map(
        body, mesh=mesh, in_specs=(spec, spec), out_specs=(spec, spec), check_vma=False
    )
```

time: 86.4 us -> 38.7 us (0.45)
  Pallas kernels: 0 us -> 34.7 us
  other arithmetic: 27.5 us -> 0 us
  waiting for transfers between devices: 24.7 us -> 0 us
  starting transfers between devices: 22.2 us -> 0 us
  local copies, waits for them, and re-layouts: 7.24 us -> 3.14 us
  between operations: 4.55 us -> 0.65 us
    pallas_call x0 -> x1, Pallas kernels: none -> 34.7 us  [body(): pl.pallas_call(kernel, out_shape=(whole, whole), in_specs=[vmem, vmem], o...]
    ppermute x18 -> x0, waiting for transfers between devices: 24.7 us -> none  [shifted(): return lax.ppermute(value, axis, pairs)]
    ppermute x18 -> x0, starting transfers between devices: 22.2 us -> none  [shifted(): return lax.ppermute(value, axis, pairs)]
    reduce_sum x97 -> x0, other arithmetic: 17.9 us -> none  [the longest x91 16.6 us: product(): jnp.sum(left_real[:, :, None] * right_real[None] - left_imag[:, :, None]...]
    add x38 -> x0, other arithmetic: 3.31 us -> none  [the longest x26 2.01 us: add_identity(): return jnp.stack([matrix[:, :, 0] + identity, matrix[:, :, 1]], axis=2)]
    slice x89 -> x0, local copies, waits for them, and re-layouts: 2.81 us -> none  [the longest x2 0.82 us: body(): field = [gauge_links[direction] for direction in range(4)]]
    another operation x73 -> x0, other arithmetic: 2.7 us -> none  [the longest x16 0.96 us: product(): return jnp.stack([real_part, imag_part], axis=2)]
    mul x49 -> x0, other arithmetic: 1.83 us -> none  [the longest x29 1.18 us: product(): left_imag[:, :, None] * right_imag[None]]
  transfers between devices with their start and end apart: 18 -> 0, of which waited for: 11 -> 0; matrix products, arithmetic and copies ran while one was open for 10% -> 0% of each run, Pallas kernels for 0% -> 0%
where the time goes in v1:
time: 38.7 us; the launch traced here: 38.5 us
  Pallas kernels  34.7 us (90%)
  local copies, waits for them, and re-layouts  3.14 us (8%)
  between operations  0.65 us (2%)
    pallas_call x1, Pallas kernels, body(): pl.pallas_call(kernel, out_shape=(whole, whole), in_specs=[vmem, vmem], o...  34.7 us
    unnamed x6, local copies, waits for them, and re-layouts  3.14 us

profile of v1, /device:TPU:0, one launch (start us, length us, event | category | flops | bytes accessed | tf_op | source)
XLA Modules:
  0.0 38.5 jit_solution(8111134732776945542)
XLA Ops:
  0.6 0.0 copy-start
  0.6 0.9 %copy-done = f32[4,3,3,2,2,2,1,128]{7,6,5,4,3,2,1,0:T(1,128)S(1)} copy-done((f32[4,3,3,2,2,2,1,128]{7,6,5,4,3,2,1,0:T(1,128)S(1)}, f32[4,3,3,2,2,2,1,128]{7,6,5,4,3,2,1,0:T(1,128)}, u32[]{:S(2)}) %copy-start) | copy-done | bytes 147480
  1.5 0.0 copy-start.1
  1.5 0.9 %copy-done.1 = f32[4,3,3,2,2,2,1,128]{7,6,5,4,3,2,1,0:T(1,128)S(1)} copy-done((f32[4,3,3,2,2,2,1,128]{7,6,5,4,3,2,1,0:T(1,128)S(1)}, f32[4,3,3,2,2,2,1,128]{7,6,5,4,3,2,1,0:T(1,128)}, u32[]{:S(2)}) %copy-start.1) | copy-done | bytes 147480
  2.5 34.7 %shard_map.41 = (f32[4,18,4,128]{3,2,1,0:T(4,128)S(1)}, f32[4,18,4,128]{3,2,1,0:T(4,128)S(1)}) custom-call(f32[4,18,4,128]{3,2,1,0:T(4,128)S(1)} %bitcast.8, f32[4,18,4,128]{3,2,1,0:T(4,128)S(1)} %bitcast.9), custom_call_target="tpu_custom_call" | custom-call | tf_op jit(solution)/shard_map/pallas_call | solution.py:335
  37.2 0.7 %copy.8 = f32[4,3,3,2,2,2,1,128]{7,6,5,4,3,2,1,0:T(1,128)} copy(f32[4,3,3,2,2,2,1,128]{7,6,5,4,3,2,1,0:T(1,128)S(1)} %bitcast.11) | data formatting | bytes 294912
  37.8 0.7 %copy.9 = f32[4,3,3,2,2,2,1,128]{7,6,5,4,3,2,1,0:T(1,128)} copy(f32[4,3,3,2,2,2,1,128]{7,6,5,4,3,2,1,0:T(1,128)S(1)} %bitcast.10) | data formatting | bytes 294912
Async XLA Ops:
  0.6 0.9 %copy-start = (f32[4,3,3,2,2,2,1,128]{7,6,5,4,3,2,1,0:T(1,128)S(1)}, f32[4,3,3,2,2,2,1,128]{7,6,5,4,3,2,1,0:T(1,128)}, u32[]{:S(2)}) copy-start(f32[4,3,3,2,2,2,1,128]{7,6,5,4,3,2,1,0:T(1,128)} %param.2) | copy-start | bytes 442372
  1.5 0.9 %copy-start.1 = (f32[4,3,3,2,2,2,1,128]{7,6,5,4,3,2,1,0:T(1,128)S(1)}, f32[4,3,3,2,2,2,1,128]{7,6,5,4,3,2,1,0:T(1,128)}, u32[]{:S(2)}) copy-start(f32[4,3,3,2,2,2,1,128]{7,6,5,4,3,2,1,0:T(1,128)} %param.3) | copy-start | bytes 442372

commit v2 on v1

--- a/solution.py
+++ b/solution.py
@@ -9,6 +9,7 @@
 STEP = 0.25
 AXES = ("gx", "gy", "gz")
 MESH = pl.DeviceIdType.MESH
+EDGES = ((1, 2), (2, 1))
 
 MOMENT_PLANES = (2, 4, 10, 3, 5, 11, 1, 9)
 
@@ -138,21 +139,30 @@
 
 def kernel(
     links_in, moment_in, links_out, moment_out,
-    field, halo, moment, moment_halo, kicks, kicks_in, local, operands, results,
-    field_send, field_recv, moment_send, moment_recv, kick_send, kick_recv,
+    field, halo, moment, partial, moment_halo, kicks, kicks_in, edge_out, edge_in, operands, results,
+    field_send, field_recv, moment_send, moment_recv, kick_send, kick_recv, edge_send, edge_recv,
 ):
     coords = [lax.axis_index(axis) for axis in AXES]
     counts = [lax.axis_size(axis) for axis in AXES]
 
+    def displaced(*moves):
+        place = list(coords)
+        for axis, steps in moves:
+            place[axis] = lax.rem(coords[axis] + (steps + counts[axis]), counts[axis])
+        return tuple(place)
+
     def neighbour(axis, steps):
-        place = list(coords)
-        place[axis] = lax.rem(coords[axis] + (steps + counts[axis]), counts[axis])
-        return tuple(place)
+        return displaced((axis, steps))
 
     barrier = pltpu.get_barrier_semaphore()
     for axis in range(3):
         for steps in (-1, 1):
             pl.semaphore_signal(barrier, inc=1, device_id=neighbour(axis, steps), device_id_type=MESH)
+
+    for behind, along in EDGES:
+        pl.semaphore_signal(
+            barrier, inc=1, device_id=displaced((along, 1), (behind, -1)), device_id_type=MESH
+        )
 
     for half in range(2):
         field[half] = jnp.concatenate([links_in[2 * half], links_in[2 * half + 1]], axis=1)
@@ -160,18 +170,18 @@
             moment[half, plane] = jnp.concatenate(
                 [moment_in[2 * half, source], moment_in[2 * half + 1, source]], axis=0
             )
-    pl.semaphore_wait(barrier, 6)
+    pl.semaphore_wait(barrier, 8)
 
     def field_copy(axis):
         return pltpu.make_async_remote_copy(
-            src_ref=field, dst_ref=halo.at[axis],
+            src_ref=field.at[:, pl.ds(0, 12)], dst_ref=halo.at[axis, :, pl.ds(0, 12)],
             send_sem=field_send.at[axis], recv_sem=field_recv.at[axis],
             device_id=neighbour(axis, -1), device_id_type=MESH,
         )
 
     def moment_copy(repeat, axis):
         return pltpu.make_async_remote_copy(
-            src_ref=moment, dst_ref=moment_halo.at[repeat, axis],
+            src_ref=moment if axis == 0 else partial, dst_ref=moment_halo.at[repeat, axis],
             send_sem=moment_send.at[repeat, axis], recv_sem=moment_recv.at[repeat, axis],
             device_id=neighbour(axis, -1), device_id_type=MESH,
         )
@@ -181,6 +191,14 @@
             src_ref=kicks.at[axis], dst_ref=kicks_in.at[repeat, axis],
             send_sem=kick_send.at[repeat, axis], recv_sem=kick_recv.at[repeat, axis],
             device_id=neighbour(axis, 1), device_id_type=MESH,
+        )
+
+    def edge_copy(repeat, number):
+        behind, along = EDGES[number]
+        return pltpu.make_async_remote_copy(
+            src_ref=edge_out.at[number], dst_ref=edge_in.at[repeat, number],
+            send_sem=edge_send.at[repeat, number], recv_sem=edge_recv.at[repeat, number],
+            device_id=displaced((along, 1), (behind, -1)), device_id_type=MESH,
         )
 
     for axis in (2, 1, 0):
@@ -252,63 +270,99 @@
         zero = jnp.zeros((8, 8, 128), jnp.float32)
         nu_a, nu_b, nu_c = results[0, 2], results[1, 2], results[2, 2]
         mu_a, mu_b, mu_c = results[0, 1], results[1, 1], results[2, 1]
+        flip_nu_b = flip(nu_b)
+        kicks[0, 0] = select(top, zero, flip(nu_c))
+        kicks[0, 1] = select(top, nu_a, flip_nu_b)
+        kick_copy(repeat, 0).start()
         kicks[2, 0] = select(top, mu_a, mu_b)
         kicks[2, 1] = select(top, zero, nu_c)
+        kicks[1, 0] = select(top, mu_c, zero)
+        kicks[1, 1] = select(top, flip_nu_b, nu_a)
+        kick_copy(repeat, 1).start()
         kick_copy(repeat, 2).start()
-        nu_b = flip(nu_b)
-        kicks[1, 0] = select(top, mu_c, zero)
-        kicks[1, 1] = select(top, nu_b, nu_a)
-        kick_copy(repeat, 1).start()
-        kicks[0, 0] = select(top, zero, flip(nu_c))
-        kicks[0, 1] = select(top, nu_a, nu_b)
-        kick_copy(repeat, 0).start()
+
+        @pl.when(repeat < 2)
+        def _():
+            for number, (_, along) in enumerate(EDGES):
+                edge_out[number] = select(top, kicks[along, 0], kicks[along, 1])
+                edge_copy(repeat, number).start()
+
         p_a, p_b, p_c = results[0, 0], results[1, 0], results[2, 0]
         q_c = flip(p_c)
-        local[0] = (
-            p_a + p_b + select(top, p_c, -q_c) + pltpu.roll(select(top, mu_b, mu_a), 1, 2)
-        )
-        local[1] = (
+        here = (
+            p_a + p_b + select(top, p_c, -q_c) + pltpu.roll(select(top, mu_b, mu_a), 1, 2),
             select(top, q_c, -p_c) - p_a - flip(p_b)
-            + pltpu.roll(select(top, flip(mu_c), zero), 1, 2)
-        )
+            + pltpu.roll(select(top, flip(mu_c), zero), 1, 2),
+        )
+        factor = jnp.where(repeat == 1, STEP * BETA / 3.0, 0.5 * STEP * BETA / 3.0)
+        for half in range(2):
+            partial[half] = moment[half] - factor * (
+                here[half] + swap_y(select(near_y, kicks[1, half], zero))
+            )
         kick_copy(repeat, 0).wait()
         for half in range(2):
-            local[half] += swap_x(select(near_x, kicks[0, half], kicks_in[repeat, 0, half]))
-        kick_copy(repeat, 1).wait()
-        for half in range(2):
-            local[half] += swap_y(select(near_y, kicks[1, half], kicks_in[repeat, 1, half]))
-        kick_copy(repeat, 2).wait()
-        factor = jnp.where(repeat == 1, STEP * BETA / 3.0, 0.5 * STEP * BETA / 3.0)
-        for half in range(2):
-            moment[half] = moment[half] - factor * (local[half] + kicks_in[repeat, 2, half])
+            partial[half] -= factor * swap_x(
+                select(near_x, kicks[0, half], kicks_in[repeat, 0, half])
+            )
 
         @pl.when(repeat < 2)
         def _():
-            for axis in (2, 1, 0):
+            for axis in (1, 2):
                 moment_copy(repeat, axis).start()
+
+        def arrival(along, value):
+            if along == 1:
+                return swap_y(select(near_y, zero, value))
+            return value
+
+        for along in (2, 1):
+            kick_copy(repeat, along).wait()
+        for half in range(2):
+            moment[half] = partial[half] - factor * (
+                arrival(1, kicks_in[repeat, 1, half])
+                + kicks_in[repeat, 2, half]
+            )
+
+        @pl.when(repeat < 2)
+        def _():
+            moment_copy(repeat, 0).start()
 
             def own(half, carry):
                 advance(moment.at[half], field.at[half])
                 return carry
 
             lax.fori_loop(0, 2, own, 0)
-
-            def arrived(axis, carry):
+            for axis in range(3):
                 moment_copy(repeat, axis).wait()
+                if axis > 0:
+                    edge_copy(repeat, axis - 1).wait()
+                    edge = edge_in[repeat, axis - 1]
+                    edges = (select(top, edge, zero), select(top, zero, edge))
+                    for half in range(2):
+                        moment_halo[repeat, axis, half] -= factor * (
+                            arrival(axis, kicks[axis, half])
+                            + arrival(3 - axis, edges[half])
+                        )
 
                 def ahead(half, carry):
                     advance(moment_halo.at[repeat, axis, half], halo.at[axis, half])
                     return carry
 
-                return lax.fori_loop(0, 2, ahead, carry)
-
-            for axis in range(3):
-                arrived(axis, 0)
+                lax.fori_loop(0, 2, ahead, 0)
 
         return carry
 
     for axis in range(3):
         field_copy(axis).wait()
+
+        for half in range(2):
+            for column, (one, two) in enumerate(((1, 2), (2, 0), (0, 1))):
+                ar, ai = halo[axis, half, 2 * one], halo[axis, half, 2 * one + 1]
+                br, bi = halo[axis, half, 6 + 2 * two], halo[axis, half, 7 + 2 * two]
+                cr, ci = halo[axis, half, 2 * two], halo[axis, half, 2 * two + 1]
+                dr, di = halo[axis, half, 6 + 2 * one], halo[axis, half, 7 + 2 * one]
+                halo[axis, half, 12 + 2 * column] = ar * br - ai * bi - cr * dr + ci * di
+                halo[axis, half, 13 + 2 * column] = cr * di + ci * dr - ar * bi - ai * br
     lax.fori_loop(0, 3, round_of, 0)
 
     for half in range(2):
@@ -341,10 +395,12 @@
             pltpu.VMEM((2, 18, 8, 128), jnp.float32),
             pltpu.VMEM((3, 2, 18, 8, 128), jnp.float32),
             pltpu.VMEM((2, 8, 8, 128), jnp.float32),
+            pltpu.VMEM((2, 8, 8, 128), jnp.float32),
             pltpu.VMEM((2, 3, 2, 8, 8, 128), jnp.float32),
             pltpu.VMEM((3, 2, 8, 8, 128), jnp.float32),
             pltpu.VMEM((3, 3, 2, 8, 8, 128), jnp.float32),
             pltpu.VMEM((2, 8, 8, 128), jnp.float32),
+            pltpu.VMEM((2, 2, 8, 8, 128), jnp.float32),
             pltpu.VMEM((3, 4, 18, 8, 128), jnp.float32),
             pltpu.VMEM((3, 3, 8, 8, 128), jnp.float32),
             pltpu.SemaphoreType.DMA((3,)),
@@ -353,6 +409,8 @@
             pltpu.SemaphoreType.DMA((2, 3)),
             pltpu.SemaphoreType.DMA((3, 3)),
             pltpu.SemaphoreType.DMA((3, 3)),
+            pltpu.SemaphoreType.DMA((2, 2)),
+            pltpu.SemaphoreType.DMA((2, 2)),
         ],
         compiler_params=pltpu.CompilerParams(
             collective_id=0, has_side_effects=True, vmem_limit_bytes=16 * 1024 * 1024

time: 38.7 us -> 34.4 us (0.89)
  Pallas kernels: 34.7 us -> 30.4 us
    pallas_call x1, Pallas kernels: 34.7 us -> 30.4 us  [body(): pl.pallas_call(kernel, out_shape=(whole, whole), in_specs=[vmem, vmem], o...]
where the time goes in v2:
time: 34.4 us; the launch traced here: 34.2 us
  Pallas kernels  30.4 us (88%)
  local copies, waits for them, and re-layouts  3.14 us (9%)
  between operations  0.65 us (2%)
    pallas_call x1, Pallas kernels, body(): pl.pallas_call(kernel, out_shape=(whole, whole), in_specs=[vmem, vmem], o...  30.4 us
    unnamed x6, local copies, waits for them, and re-layouts  3.14 us

profile of v2, /device:TPU:0, one launch (start us, length us, event | category | flops | bytes accessed | tf_op | source)
XLA Modules:
  0.0 34.2 jit_solution(8418372183951939779)
XLA Ops:
  0.6 0.0 copy-start
  0.6 0.9 %copy-done = f32[4,3,3,2,2,2,1,128]{7,6,5,4,3,2,1,0:T(1,128)S(1)} copy-done((f32[4,3,3,2,2,2,1,128]{7,6,5,4,3,2,1,0:T(1,128)S(1)}, f32[4,3,3,2,2,2,1,128]{7,6,5,4,3,2,1,0:T(1,128)}, u32[]{:S(2)}) %copy-start) | copy-done | bytes 147480
  1.5 0.0 copy-start.1
  1.5 0.9 %copy-done.1 = f32[4,3,3,2,2,2,1,128]{7,6,5,4,3,2,1,0:T(1,128)S(1)} copy-done((f32[4,3,3,2,2,2,1,128]{7,6,5,4,3,2,1,0:T(1,128)S(1)}, f32[4,3,3,2,2,2,1,128]{7,6,5,4,3,2,1,0:T(1,128)}, u32[]{:S(2)}) %copy-start.1) | copy-done | bytes 147480
  2.5 30.4 %shard_map.41 = (f32[4,18,4,128]{3,2,1,0:T(4,128)S(1)}, f32[4,18,4,128]{3,2,1,0:T(4,128)S(1)}) custom-call(f32[4,18,4,128]{3,2,1,0:T(4,128)S(1)} %bitcast.8, f32[4,18,4,128]{3,2,1,0:T(4,128)S(1)} %bitcast.9), custom_call_target="tpu_custom_call" | custom-call | tf_op jit(solution)/shard_map/pallas_call | solution.py:389
  32.9 0.7 %copy.8 = f32[4,3,3,2,2,2,1,128]{7,6,5,4,3,2,1,0:T(1,128)} copy(f32[4,3,3,2,2,2,1,128]{7,6,5,4,3,2,1,0:T(1,128)S(1)} %bitcast.11) | data formatting | bytes 294912
  33.6 0.7 %copy.9 = f32[4,3,3,2,2,2,1,128]{7,6,5,4,3,2,1,0:T(1,128)} copy(f32[4,3,3,2,2,2,1,128]{7,6,5,4,3,2,1,0:T(1,128)S(1)} %bitcast.10) | data formatting | bytes 294912
Async XLA Ops:
  0.6 0.9 %copy-start = (f32[4,3,3,2,2,2,1,128]{7,6,5,4,3,2,1,0:T(1,128)S(1)}, f32[4,3,3,2,2,2,1,128]{7,6,5,4,3,2,1,0:T(1,128)}, u32[]{:S(2)}) copy-start(f32[4,3,3,2,2,2,1,128]{7,6,5,4,3,2,1,0:T(1,128)} %param.2) | copy-start | bytes 442372
  1.5 0.9 %copy-start.1 = (f32[4,3,3,2,2,2,1,128]{7,6,5,4,3,2,1,0:T(1,128)S(1)}, f32[4,3,3,2,2,2,1,128]{7,6,5,4,3,2,1,0:T(1,128)}, u32[]{:S(2)}) copy-start(f32[4,3,3,2,2,2,1,128]{7,6,5,4,3,2,1,0:T(1,128)} %param.3) | copy-start | bytes 442372

commit v3 on v2

--- a/solution.py
+++ b/solution.py
@@ -139,7 +139,7 @@
 
 def kernel(
     links_in, moment_in, links_out, moment_out,
-    field, halo, moment, partial, moment_halo, kicks, kicks_in, edge_out, edge_in, operands, results,
+    field, halo, moment, partial, moment_halo, kicks, kicks_in, edge_out, edge_in, field_y, partial_y, kicks_y, operands, results,
     field_send, field_recv, moment_send, moment_recv, kick_send, kick_recv, edge_send, edge_recv,
 ):
     coords = [lax.axis_index(axis) for axis in AXES]
@@ -174,21 +174,24 @@
 
     def field_copy(axis):
         return pltpu.make_async_remote_copy(
-            src_ref=field.at[:, pl.ds(0, 12)], dst_ref=halo.at[axis, :, pl.ds(0, 12)],
+            src_ref=field_y if axis == 1 else field.at[:, pl.ds(0, 12)],
+            dst_ref=halo.at[1, 0, pl.ds(0, 12)] if axis == 1 else halo.at[axis, :, pl.ds(0, 12)],
             send_sem=field_send.at[axis], recv_sem=field_recv.at[axis],
             device_id=neighbour(axis, -1), device_id_type=MESH,
         )
 
     def moment_copy(repeat, axis):
         return pltpu.make_async_remote_copy(
-            src_ref=moment if axis == 0 else partial, dst_ref=moment_halo.at[repeat, axis],
+            src_ref=(moment, partial_y, partial)[axis],
+            dst_ref=moment_halo.at[repeat, 1, 0] if axis == 1 else moment_halo.at[repeat, axis],
             send_sem=moment_send.at[repeat, axis], recv_sem=moment_recv.at[repeat, axis],
             device_id=neighbour(axis, -1), device_id_type=MESH,
         )
 
     def kick_copy(repeat, axis):
         return pltpu.make_async_remote_copy(
-            src_ref=kicks.at[axis], dst_ref=kicks_in.at[repeat, axis],
+            src_ref=kicks_y if axis == 1 else kicks.at[axis],
+            dst_ref=kicks_in.at[repeat, 1, 0] if axis == 1 else kicks_in.at[repeat, axis],
             send_sem=kick_send.at[repeat, axis], recv_sem=kick_recv.at[repeat, axis],
             device_id=neighbour(axis, 1), device_id_type=MESH,
         )
@@ -201,9 +204,6 @@
             device_id=displaced((along, 1), (behind, -1)), device_id_type=MESH,
         )
 
-    for axis in (2, 1, 0):
-        field_copy(axis).start()
-
     row = lax.broadcasted_iota(jnp.int32, (1, 8, 128), 1)
     top = row < 4
     near_x = lax.rem(row, 4) < 2
@@ -212,6 +212,17 @@
     def select(mask, first, second):
         return jnp.where(jnp.broadcast_to(mask, first.shape), first, second)
 
+    def pack_near(first, second):
+        return select(near_y, first, pltpu.roll(second, 1, 1))
+
+    def pack_far(first, second):
+        return select(near_y, pltpu.roll(second, 7, 1), first)
+
+    field_copy(2).start()
+    field_y[...] = pack_near(field[0, 0:12], field[1, 0:12])
+    field_copy(1).start()
+    field_copy(0).start()
+
     def flip(value):
         return pltpu.roll(value, 4, 1)
 
@@ -225,7 +236,8 @@
         return swap_x(select(near_x, halo[0, half], field[half]))
 
     def ahead_y(half):
-        return swap_y(select(near_y, halo[1, half], field[half]))
+        face = halo[1, 0] if half == 0 else pltpu.roll(halo[1, 0], 7, 1)
+        return swap_y(select(near_y, face, field[half]))
 
     def ahead_t(half):
         return pltpu.roll(field[half], 127, 2)
@@ -278,6 +290,7 @@
         kicks[2, 1] = select(top, zero, nu_c)
         kicks[1, 0] = select(top, mu_c, zero)
         kicks[1, 1] = select(top, flip_nu_b, nu_a)
+        kicks_y[...] = pack_far(kicks[1, 0], kicks[1, 1])
         kick_copy(repeat, 1).start()
         kick_copy(repeat, 2).start()
 
@@ -307,6 +320,7 @@
 
         @pl.when(repeat < 2)
         def _():
+            partial_y[...] = pack_near(partial[0], partial[1])
             for axis in (1, 2):
                 moment_copy(repeat, axis).start()
 
@@ -319,7 +333,7 @@
             kick_copy(repeat, along).wait()
         for half in range(2):
             moment[half] = partial[half] - factor * (
-                arrival(1, kicks_in[repeat, 1, half])
+                arrival(1, kicks_in[repeat, 1, 0] if half == 0 else pltpu.roll(kicks_in[repeat, 1, 0], 1, 1))
                 + kicks_in[repeat, 2, half]
             )
 
@@ -338,24 +352,27 @@
                     edge_copy(repeat, axis - 1).wait()
                     edge = edge_in[repeat, axis - 1]
                     edges = (select(top, edge, zero), select(top, zero, edge))
-                    for half in range(2):
-                        moment_halo[repeat, axis, half] -= factor * (
-                            arrival(axis, kicks[axis, half])
-                            + arrival(3 - axis, edges[half])
-                        )
+                    totals = [
+                        arrival(axis, kicks[axis, half]) + arrival(3 - axis, edges[half])
+                        for half in range(2)
+                    ]
+                    if axis == 1:
+                        totals = [pack_near(totals[0], totals[1])]
+                    for half, total in enumerate(totals):
+                        moment_halo[repeat, axis, half] -= factor * total
 
                 def ahead(half, carry):
                     advance(moment_halo.at[repeat, axis, half], halo.at[axis, half])
                     return carry
 
-                lax.fori_loop(0, 2, ahead, 0)
+                lax.fori_loop(0, 1 if axis == 1 else 2, ahead, 0)
 
         return carry
 
     for axis in range(3):
         field_copy(axis).wait()
 
-        for half in range(2):
+        for half in range(1 if axis == 1 else 2):
             for column, (one, two) in enumerate(((1, 2), (2, 0), (0, 1))):
                 ar, ai = halo[axis, half, 2 * one], halo[axis, half, 2 * one + 1]
                 br, bi = halo[axis, half, 6 + 2 * two], halo[axis, half, 7 + 2 * two]
@@ -401,6 +418,9 @@
             pltpu.VMEM((3, 3, 2, 8, 8, 128), jnp.float32),
             pltpu.VMEM((2, 8, 8, 128), jnp.float32),
             pltpu.VMEM((2, 2, 8, 8, 128), jnp.float32),
+            pltpu.VMEM((12, 8, 128), jnp.float32),
+            pltpu.VMEM((8, 8, 128), jnp.float32),
+            pltpu.VMEM((8, 8, 128), jnp.float32),
             pltpu.VMEM((3, 4, 18, 8, 128), jnp.float32),
             pltpu.VMEM((3, 3, 8, 8, 128), jnp.float32),
             pltpu.SemaphoreType.DMA((3,)),

time: 34.4 us -> 32.8 us (0.953)
  Pallas kernels: 30.4 us -> 28.8 us
    pallas_call x1, Pallas kernels: 30.4 us -> 28.8 us  [body(): pl.pallas_call(kernel, out_shape=(whole, whole), in_specs=[vmem, vmem], o...]
where the time goes in v3:
time: 32.8 us; the launch traced here: 32.6 us
  Pallas kernels  28.8 us (88%)
  local copies, waits for them, and re-layouts  3.14 us (10%)
  between operations  0.65 us (2%)
    pallas_call x1, Pallas kernels, body(): pl.pallas_call(kernel, out_shape=(whole, whole), in_specs=[vmem, vmem], o...  28.8 us
    unnamed x6, local copies, waits for them, and re-layouts  3.14 us

profile of v3, /device:TPU:0, one launch (start us, length us, event | category | flops | bytes accessed | tf_op | source)
XLA Modules:
  0.0 32.6 jit_solution(18012551422395090293)
XLA Ops:
  0.6 0.0 copy-start
  0.6 0.9 %copy-done = f32[4,3,3,2,2,2,1,128]{7,6,5,4,3,2,1,0:T(1,128)S(1)} copy-done((f32[4,3,3,2,2,2,1,128]{7,6,5,4,3,2,1,0:T(1,128)S(1)}, f32[4,3,3,2,2,2,1,128]{7,6,5,4,3,2,1,0:T(1,128)}, u32[]{:S(2)}) %copy-start) | copy-done | bytes 147480
  1.5 0.0 copy-start.1
  1.5 0.9 %copy-done.1 = f32[4,3,3,2,2,2,1,128]{7,6,5,4,3,2,1,0:T(1,128)S(1)} copy-done((f32[4,3,3,2,2,2,1,128]{7,6,5,4,3,2,1,0:T(1,128)S(1)}, f32[4,3,3,2,2,2,1,128]{7,6,5,4,3,2,1,0:T(1,128)}, u32[]{:S(2)}) %copy-start.1) | copy-done | bytes 147480
  2.5 28.8 %shard_map.41 = (f32[4,18,4,128]{3,2,1,0:T(4,128)S(1)}, f32[4,18,4,128]{3,2,1,0:T(4,128)S(1)}) custom-call(f32[4,18,4,128]{3,2,1,0:T(4,128)S(1)} %bitcast.8, f32[4,18,4,128]{3,2,1,0:T(4,128)S(1)} %bitcast.9), custom_call_target="tpu_custom_call" | custom-call | tf_op jit(solution)/shard_map/pallas_call | solution.py:406
  31.3 0.7 %copy.8 = f32[4,3,3,2,2,2,1,128]{7,6,5,4,3,2,1,0:T(1,128)} copy(f32[4,3,3,2,2,2,1,128]{7,6,5,4,3,2,1,0:T(1,128)S(1)} %bitcast.11) | data formatting | bytes 294912
  32.0 0.7 %copy.9 = f32[4,3,3,2,2,2,1,128]{7,6,5,4,3,2,1,0:T(1,128)} copy(f32[4,3,3,2,2,2,1,128]{7,6,5,4,3,2,1,0:T(1,128)S(1)} %bitcast.10) | data formatting | bytes 294912
Async XLA Ops:
  0.6 0.9 %copy-start = (f32[4,3,3,2,2,2,1,128]{7,6,5,4,3,2,1,0:T(1,128)S(1)}, f32[4,3,3,2,2,2,1,128]{7,6,5,4,3,2,1,0:T(1,128)}, u32[]{:S(2)}) copy-start(f32[4,3,3,2,2,2,1,128]{7,6,5,4,3,2,1,0:T(1,128)} %param.2) | copy-start | bytes 442372
  1.5 0.9 %copy-start.1 = (f32[4,3,3,2,2,2,1,128]{7,6,5,4,3,2,1,0:T(1,128)S(1)}, f32[4,3,3,2,2,2,1,128]{7,6,5,4,3,2,1,0:T(1,128)}, u32[]{:S(2)}) copy-start(f32[4,3,3,2,2,2,1,128]{7,6,5,4,3,2,1,0:T(1,128)} %param.3) | copy-start | bytes 442372
